TPU v7x, 512 devices: a whole 4x8x8 slice. The times are simulated.
512 devices in a mesh: outer: 64 (over z_lo, y, core), inner: 8 (over z_hi, x).
Axes of the slice: x: 4, y: 8, z: 8 (z_hi: 2, z_lo: 4; z = z_hi * 4 + z_lo), core: 2. Of those that a mesh axis runs over, the one named last changes fastest.
Arguments:
- queries: bfloat16 [98304, 1024], P(('outer', 'inner')), may hold values from -8 to 8
- keys: bfloat16 [98304, 1024], P(('outer', 'inner')), may hold values from -6 to 6
- values: bfloat16 [98304, 1024], P(('outer', 'inner')), may hold values from -6 to 6
- d_out: bfloat16 [98304, 1024], P(('outer', 'inner')), may hold values from -6 to 6
Outputs:
- attended: bfloat16 [98304, 1024], P(('outer', 'inner'))
- d_queries: bfloat16 [98304, 1024], P(('outer', 'inner'))
- d_keys: bfloat16 [98304, 1024], P(('outer', 'inner'))
- d_values: bfloat16 [98304, 1024], P(('outer', 'inner'))
All inputs are finite; a program needn't handle non-finite values.
Results may differ from a plain program's by a relative error of at most 0.01.
Values may be sent and summed in bfloat16 or wider, within the bound.
A program may use at most 64 MiB of HBM per device.

v0:
```python
import jax
import jax.numpy as jnp
from jax import lax
from jax.sharding import PartitionSpec as P

HEADS = 8
HEAD_DIM = 128
HOPS = 4


def from_behind(shard, axis, by):
    size = lax.axis_size(axis)
    pairs = [(i, i + by) for i in range(size) if 0 <= i + by < size]
    return lax.ppermute(shard, axis, pairs)


def padded(block, sides, width):
    for axis, dim in sides:
        count = lax.axis_size(axis)
        forward = [(i, i + 1) for i in range(count - 1)]
        forward.append((count - 1, 0))
        backward = [(target, source) for source, target in forward]
        low = lax.ppermute(
            lax.slice_in_dim(block, block.shape[dim] - width, None, axis=dim), axis, forward
        )
        high = lax.ppermute(lax.slice_in_dim(block, 0, width, axis=dim), axis, backward)
        block = jnp.concatenate([low, block, high], axis=dim)
    return block


def passed_along(shard, axis, by):
    size = lax.axis_size(axis)
    return lax.ppermute(shard, axis, [(i, (i + by) % size) for i in range(size)])


def reach_back(kv_block, stack_axis):
    gathered = [kv_block]
    current = kv_block
    for hop in range(1, HOPS):
        current = from_behind(current, "outer", 1)
        gathered.append(current)
    return jnp.stack(gathered, stack_axis)


def head_step(head_idx, state, queries, key_all, value_all, d_out, key_live):
    scale = HEAD_DIM ** (-0.5)
    start = head_idx * HEAD_DIM

    def column_piece(arr):
        return lax.dynamic_slice_in_dim(arr, start, HEAD_DIM, 1)

    q_head = column_piece(queries)
    k_head = column_piece(key_all)
    v_head = column_piece(value_all)
    g_head = column_piece(d_out)
    scores = (
        lax.dot_general(
            q_head, k_head, (((1,), (1,)), ((), ())), preferred_element_type=jnp.float32
        )
        * scale
    )
    scores = jnp.where(key_live[None, :], scores, -1e30)
    highest = jnp.max(scores, axis=1, keepdims=True)
    expo = jnp.exp(scores - highest)
    attn_weight = expo / jnp.sum(expo, axis=1, keepdims=True)
    weight_b = attn_weight.astype(jnp.bfloat16)
    out_head = jnp.dot(weight_b, v_head, preferred_element_type=jnp.float32).astype(jnp.bfloat16)
    delta = jnp.sum(
        g_head.astype(jnp.float32) * out_head.astype(jnp.float32), axis=1, keepdims=True
    )
    dprob = lax.dot_general(
        g_head, v_head, (((1,), (1,)), ((), ())), preferred_element_type=jnp.float32
    )
    dscore = (attn_weight * (dprob - delta)).astype(jnp.bfloat16)
    dq_head = (jnp.dot(dscore, k_head, preferred_element_type=jnp.float32) * scale).astype(
        jnp.bfloat16
    )
    dv_head = lax.dot_general(
        weight_b, g_head, (((0,), (0,)), ((), ())), preferred_element_type=jnp.float32
    ).astype(jnp.bfloat16)
    dk_head = (
        lax.dot_general(
            dscore, q_head, (((0,), (0,)), ((), ())), preferred_element_type=jnp.float32
        )
        * scale
    ).astype(jnp.bfloat16)
    out_all, dq_all, dk_all, dv_all = state
    return (
        lax.dynamic_update_slice_in_dim(out_all, out_head, start, 1),
        lax.dynamic_update_slice_in_dim(dq_all, dq_head, start, 1),
        lax.dynamic_update_slice_in_dim(dk_all, dk_head, start, 1),
        lax.dynamic_update_slice_in_dim(dv_all, dv_head, start, 1),
    )


def on_device(queries, keys, values, d_out):
    row_count, feat_width = queries.shape
    kv_pair = jnp.stack([keys, values])
    kv_band = padded(kv_pair, (("inner", 1),), row_count)
    kv_span = reach_back(kv_band, 0)
    key_all = kv_span[:, 0].reshape(-1, feat_width)
    value_all = kv_span[:, 1].reshape(-1, feat_width)
    outer_idx = lax.axis_index("outer")
    live_hops = outer_idx - jnp.arange(HOPS, dtype=jnp.int32) >= 0
    key_live = jnp.broadcast_to(live_hops[:, None], (HOPS, 3 * row_count)).reshape(-1)
    key_count = key_all.shape[0]
    state = (
        jnp.zeros((row_count, feat_width), jnp.bfloat16),
        jnp.zeros((row_count, feat_width), jnp.bfloat16),
        jnp.zeros((key_count, feat_width), jnp.bfloat16),
        jnp.zeros((key_count, feat_width), jnp.bfloat16),
    )

    def loop_body(head_idx, carried):
        return head_step(head_idx, carried, queries, key_all, value_all, d_out, key_live)

    attended, d_query, part_k, part_v = lax.fori_loop(0, HEADS, loop_body, state)
    grad_parts = jnp.stack(
        [
            part_k.reshape(HOPS, 3, row_count, feat_width),
            part_v.reshape(HOPS, 3, row_count, feat_width),
        ],
        1,
    )
    homed = [grad_parts[0]] + [
        from_behind(grad_parts[hop], "outer", -hop) for hop in range(1, HOPS)
    ]
    hop_total = jnp.sum(jnp.stack(homed).astype(jnp.float32), axis=0)
    grad_total = hop_total[:, 1]
    for column, offset in ((0, -1), (2, 1)):
        grad_total = grad_total + passed_along(hop_total[:, column], "inner", offset)
    return (
        attended,
        d_query,
        grad_total[0].astype(jnp.bfloat16),
        grad_total[1].astype(jnp.bfloat16),
    )


def solution(mesh):
    placed = (
        P(("outer", "inner"), None),
        P(("outer", "inner"), None),
        P(("outer", "inner"), None),
        P(("outer", "inner"), None),
    )
    return jax.shard_map(
        on_device,
        mesh=mesh,
        in_specs=placed,
        out_specs=(
            P(("outer", "inner"), None),
            P(("outer", "inner"), None),
            P(("outer", "inner"), None),
            P(("outer", "inner"), None),
        ),
        check_vma=False,
    )
```

profile of v0, /device:TPU:121, one launch (start us, length us, event | category | flops | bytes accessed | tf_op | source)
XLA Modules:
  0.0 499.5 jit_solution(6842545137496413508)
XLA Ops:
  1.8 11.9 %collective-permute-start.1 = (bf16[2,192,1024]{2,1,0:T(8,128)(2,1)S(1)}, bf16[2,192,1024]{2,1,0:T(8,128)(2,1)S(1)}, u32[]{:S(2)}, u32[]{:S(2)}) collective-permute-start(bf16[2,192,1024]{2,1,0:T(8,128)(2,1)S(1)} %pad_maximum_fusion.3), channel_id=1, source_target_pairs={{1,0},{2,1},{3,2},{4,3},{5,4},{6,5},{7,6},{0,7},{9,8},{10,9},{11,1... | collective-permute-start | bytes 2359304 | tf_op jit(solution)/shard_map/ppermute | solution.py:26
  13.8 1.9 collective-permute-start
  15.7 30.1 %collective-permute-done.1 = bf16[2,192,1024]{2,1,0:T(8,128)(2,1)S(1)} collective-permute-done((bf16[2,192,1024]{2,1,0:T(8,128)(2,1)S(1)}, bf16[2,192,1024]{2,1,0:T(8,128)(2,1)S(1)}, u32[]{:S(2)}, u32[]{:S(2)}) %collective-permute-start.1) | collective-permute-done | bytes 786464 | tf_op jit(solution)/shard_map/ppermute | solution.py:26
  45.8 9.9 %collective-permute-done = bf16[2,192,1024]{2,1,0:T(8,128)(2,1)S(1)} collective-permute-done((bf16[2,192,1024]{2,1,0:T(8,128)(2,1)S(1)}, bf16[2,192,1024]{2,1,0:T(8,128)(2,1)S(1)}, u32[]{:S(2)}, u32[]{:S(2)}) %collective-permute-start) | collective-permute-done | bytes 786464 | tf_op jit(solution)/shard_map/ppermute | solution.py:23
  55.7 2.8 fusion.39
  58.5 2.7 collective-permute-start.2
  61.2 25.8 %collective-permute-done.2 = bf16[2,576,1024]{2,1,0:T(8,128)(2,1)S(1)} collective-permute-done((bf16[2,576,1024]{2,1,0:T(8,128)(2,1)S(1)}, bf16[2,576,1024]{2,1,0:T(8,128)(2,1)S(1)}, u32[]{:S(2)}, u32[]{:S(2)}) %collective-permute-start.2) | collective-permute-done | bytes 2359328 | tf_op jit(solution)/shard_map/ppermute | solution.py:14
  86.9 6.5 %collective-permute-start.3 = (bf16[2,576,1024]{2,1,0:T(8,128)(2,1)S(1)}, bf16[2,576,1024]{2,1,0:T(8,128)(2,1)}, u32[]{:S(2)}, u32[]{:S(2)}) collective-permute-start(bf16[2,576,1024]{2,1,0:T(8,128)(2,1)S(1)} %collective-permute-done.2), channel_id=1, source_target_pairs={{0,8},{8,16},{16,24},{24,32},{32,40},{40,48},{48,56},{56,64},{64,7... | collective-permute-start | bytes 7077896 | tf_op jit(solution)/shard_map/ppermute | solution.py:14
  93.4 25.8 %collective-permute-done.3 = bf16[2,576,1024]{2,1,0:T(8,128)(2,1)} collective-permute-done((bf16[2,576,1024]{2,1,0:T(8,128)(2,1)S(1)}, bf16[2,576,1024]{2,1,0:T(8,128)(2,1)}, u32[]{:S(2)}, u32[]{:S(2)}) %collective-permute-start.3) | collective-permute-done | bytes 2359328 | tf_op jit(solution)/shard_map/ppermute | solution.py:14
  119.2 6.6 %collective-permute-start.4 = (bf16[2,576,1024]{2,1,0:T(8,128)(2,1)}, bf16[2,576,1024]{2,1,0:T(8,128)(2,1)}, u32[]{:S(2)}, u32[]{:S(2)}) collective-permute-start(bf16[2,576,1024]{2,1,0:T(8,128)(2,1)} %collective-permute-done.3), channel_id=1, source_target_pairs={{0,8},{8,16},{16,24},{24,32},{32,40},{40,48},{48,56},{56,64},{64,7... | collective-permute-start | bytes 7077896 | tf_op jit(solution)/shard_map/ppermute | solution.py:14
  125.8 26.1 %collective-permute-done.4 = bf16[2,576,1024]{2,1,0:T(8,128)(2,1)} collective-permute-done((bf16[2,576,1024]{2,1,0:T(8,128)(2,1)}, bf16[2,576,1024]{2,1,0:T(8,128)(2,1)}, u32[]{:S(2)}, u32[]{:S(2)}) %collective-permute-start.4) | collective-permute-done | bytes 2359328 | tf_op jit(solution)/shard_map/ppermute | solution.py:14
  151.9 4.7 pad_maximum_fusion
  156.6 4.7 fusion.41
  161.4 2.7 broadcast.42.clone
  164.1 2.8 broadcast.42
  167.0 99.0 %while.20 = (s32[]{:T(128)}, bf16[192,1024]{1,0:T(8,128)(2,1)S(1)}, bf16[192,1024]{1,0:T(8,128)(2,1)S(1)}, bf16[2304,1024]{1,0:T(8,128)(2,1)}, bf16[2304,1024]{1...) while((s32[]{:T(128)}, bf16[192,1024]{1,0:T(8,128)(2,1)S(1)}, ...), condition=%wide.region_4.5_spmd.clone, body=%wide.region_0.4_spmd.clone.sunk | while | flops 687611328 | bytes 15507387 | solution.py:117
  171.6 1.7 fusion.68
  174.8 2.3 fusion.71
  177.1 2.2 fusion.70
  184.0 1.7 fusion.68
  187.1 2.3 fusion.71
  189.5 2.2 fusion.70
  196.4 1.7 fusion.68
  199.6 2.3 fusion.71
  201.9 2.2 fusion.70
  208.8 1.7 fusion.68
  211.9 2.3 fusion.71
  214.2 2.2 fusion.70
  224.2 2.4 fusion.71
  226.6 2.2 fusion.70
  236.6 2.3 fusion.71
  239.0 2.2 fusion.70
  245.8 1.7 fusion.68
  249.0 2.4 fusion.71
  251.4 2.2 fusion.70
  261.4 2.3 fusion.71
  263.7 2.2 fusion.70
  265.9 4.7 fusion.32
  270.6 2.2 collective-permute-start.5
  272.8 2.9 collective-permute-start.7
  275.7 3.0 collective-permute-start.6
  278.7 57.4 %collective-permute-done.5 = bf16[2,3,192,1024]{3,2,1,0:T(8,128)(2,1)S(1)} collective-permute-done((bf16[2,3,192,1024]{3,2,1,0:T(8,128)(2,1)S(1)}, bf16[2,3,192,1024]{3,2,1,0:T(8,128)(2,1)S(1)}, u32[]{:S(2)}, u32[]{:S(2)}) %collective-permute-start.5) | collective-permute-done | bytes 2359328 | tf_op jit(solution)/shard_map/ppermute | solution.py:14
  336.1 49.4 %collective-permute-done.7 = bf16[2,3,192,1024]{3,2,1,0:T(8,128)(2,1)S(1)} collective-permute-done((bf16[2,3,192,1024]{3,2,1,0:T(8,128)(2,1)S(1)}, bf16[2,3,192,1024]{3,2,1,0:T(8,128)(2,1)S(1)}, u32[]{:S(2)}, u32[]{:S(2)}) %collective-permute-start.7) | collective-permute-done | bytes 2359328 | tf_op jit(solution)/shard_map/ppermute | solution.py:14
  385.5 21.4 %collective-permute-done.6 = bf16[2,3,192,1024]{3,2,1,0:T(8,128)(2,1)S(1)} collective-permute-done((bf16[2,3,192,1024]{3,2,1,0:T(8,128)(2,1)S(1)}, bf16[2,3,192,1024]{3,2,1,0:T(8,128)(2,1)S(1)}, u32[]{:S(2)}, u32[]{:S(2)}) %collective-permute-start.6) | collective-permute-done | bytes 2359328 | tf_op jit(solution)/shard_map/ppermute | solution.py:14
  406.9 2.5 convert_reduce_fusion
  409.7 1.9 collective-permute-start.8
  411.7 3.4 collective-permute-start.9
  415.0 82.9 %collective-permute-done.8 = f32[2,192,1024]{2,1,0:T(8,128)S(1)} collective-permute-done((f32[2,192,1024]{2,1,0:T(8,128)S(1)}, f32[2,192,1024]{2,1,0:T(8,128)S(1)}, u32[]{:S(2)}, u32[]{:S(2)}) %collective-permute-start.8) | collective-permute-done | bytes 1572896 | tf_op jit(solution)/shard_map/ppermute | solution.py:33
  (73 shorter events, 57.4 us)
Async XLA Ops:
  1.8 44.0 %collective-permute-start.1 = (bf16[2,192,1024]{2,1,0:T(8,128)(2,1)S(1)}, bf16[2,192,1024]{2,1,0:T(8,128)(2,1)S(1)}, u32[]{:S(2)}, u32[]{:S(2)}) collective-permute-start(bf16[2,192,1024]{2,1,0:T(8,128)(2,1)S(1)} %pad_maximum_fusion.3), channel_id=1, source_target_pairs={{1,0},{2,1},{3,2},{4,3},{5,4},{6,5},{7,6},{0,7},{9,8},{10,9},{11,1... | collective-permute-start | bytes 2359304 | tf_op jit(solution)/shard_map/ppermute | solution.py:26
  13.8 41.9 %collective-permute-start = (bf16[2,192,1024]{2,1,0:T(8,128)(2,1)S(1)}, bf16[2,192,1024]{2,1,0:T(8,128)(2,1)S(1)}, u32[]{:S(2)}, u32[]{:S(2)}) collective-permute-start(bf16[2,192,1024]{2,1,0:T(8,128)(2,1)S(1)} %pad_maximum_fusion.3), channel_id=1, source_target_pairs={{0,1},{1,2},{2,3},{3,4},{4,5},{5,6},{6,7},{7,0},{8,9},{9,10},{10,1... | collective-permute-start | bytes 2359304 | tf_op jit(solution)/shard_map/ppermute | solution.py:23
  58.5 28.5 %collective-permute-start.2 = (bf16[2,576,1024]{2,1,0:T(8,128)(2,1)S(1)}, bf16[2,576,1024]{2,1,0:T(8,128)(2,1)S(1)}, u32[]{:S(2)}, u32[]{:S(2)}) collective-permute-start(bf16[2,576,1024]{2,1,0:T(8,128)(2,1)S(1)} %get-tuple-element.236), channel_id=1, source_target_pairs={{0,8},{8,16},{16,24},{24,32},{32,40},{40,48},{48,56},{56,64},{64,7... | collective-permute-start | bytes 7077896 | tf_op jit(solution)/shard_map/ppermute | solution.py:14
  86.9 64.9 %copy-start = (bf16[2,576,1024]{2,1,0:T(8,128)(2,1)}, bf16[2,576,1024]{2,1,0:T(8,128)(2,1)S(1)}, u32[]{:S(2)}) copy-start(bf16[2,576,1024]{2,1,0:T(8,128)(2,1)S(1)} %collective-permute-done.2) | copy-start | bytes 7077892
  86.9 32.3 %collective-permute-start.3 = (bf16[2,576,1024]{2,1,0:T(8,128)(2,1)S(1)}, bf16[2,576,1024]{2,1,0:T(8,128)(2,1)}, u32[]{:S(2)}, u32[]{:S(2)}) collective-permute-start(bf16[2,576,1024]{2,1,0:T(8,128)(2,1)S(1)} %collective-permute-done.2), channel_id=1, source_target_pairs={{0,8},{8,16},{16,24},{24,32},{32,40},{40,48},{48,56},{56,64},{64,7... | collective-permute-start | bytes 7077896 | tf_op jit(solution)/shard_map/ppermute | solution.py:14
  119.2 32.7 %collective-permute-start.4 = (bf16[2,576,1024]{2,1,0:T(8,128)(2,1)}, bf16[2,576,1024]{2,1,0:T(8,128)(2,1)}, u32[]{:S(2)}, u32[]{:S(2)}) collective-permute-start(bf16[2,576,1024]{2,1,0:T(8,128)(2,1)} %collective-permute-done.3), channel_id=1, source_target_pairs={{0,8},{8,16},{16,24},{24,32},{32,40},{40,48},{48,56},{56,64},{64,7... | collective-permute-start | bytes 7077896 | tf_op jit(solution)/shard_map/ppermute | solution.py:14
  265.9 4.7 copy-start.1
  265.9 4.7 copy-start.2
  270.6 65.5 %collective-permute-start.5 = (bf16[2,3,192,1024]{3,2,1,0:T(8,128)(2,1)S(1)}, bf16[2,3,192,1024]{3,2,1,0:T(8,128)(2,1)S(1)}, u32[]{:S(2)}, u32[]{:S(2)}) collective-permute-start(bf16[2,3,192,1024]{3,2,1,0:T(8,128)(2,1)S(1)} %get-tuple-element.228), channel_id=1, source_target_pairs={{8,0},{16,8},{24,16},{32,24},{40,32},{48,40},{56,48},{64,56},{72,6... | collective-permute-start | bytes 7077896 | tf_op jit(solution)/shard_map/ppermute | solution.py:14
  272.8 112.7 %collective-permute-start.7 = (bf16[2,3,192,1024]{3,2,1,0:T(8,128)(2,1)S(1)}, bf16[2,3,192,1024]{3,2,1,0:T(8,128)(2,1)S(1)}, u32[]{:S(2)}, u32[]{:S(2)}) collective-permute-start(bf16[2,3,192,1024]{3,2,1,0:T(8,128)(2,1)S(1)} %get-tuple-element.229), channel_id=1, source_target_pairs={{24,0},{32,8},{40,16},{48,24},{56,32},{64,40},{72,48},{80,56},{88,... | collective-permute-start | bytes 7077896 | tf_op jit(solution)/shard_map/ppermute | solution.py:14
  275.7 131.1 %collective-permute-start.6 = (bf16[2,3,192,1024]{3,2,1,0:T(8,128)(2,1)S(1)}, bf16[2,3,192,1024]{3,2,1,0:T(8,128)(2,1)S(1)}, u32[]{:S(2)}, u32[]{:S(2)}) collective-permute-start(bf16[2,3,192,1024]{3,2,1,0:T(8,128)(2,1)S(1)} %get-tuple-element.230), channel_id=1, source_target_pairs={{16,0},{24,8},{32,16},{40,24},{48,32},{56,40},{64,48},{72,56},{80,... | collective-permute-start | bytes 7077896 | tf_op jit(solution)/shard_map/ppermute | solution.py:14
  409.7 88.2 %collective-permute-start.8 = (f32[2,192,1024]{2,1,0:T(8,128)S(1)}, f32[2,192,1024]{2,1,0:T(8,128)S(1)}, u32[]{:S(2)}, u32[]{:S(2)}) collective-permute-start(f32[2,192,1024]{2,1,0:T(8,128)S(1)} %get-tuple-element.233), channel_id=1, source_target_pairs={{0,7},{1,0},{2,1},{3,2},{4,3},{5,4},{6,5},{7,6},{8,15},{9,8},{10,9... | collective-permute-start | bytes 4718600 | tf_op jit(solution)/shard_map/ppermute | solution.py:33
  411.7 86.3 %collective-permute-start.9 = (f32[2,192,1024]{2,1,0:T(8,128)S(1)}, f32[2,192,1024]{2,1,0:T(8,128)S(1)}, u32[]{:S(2)}, u32[]{:S(2)}) collective-permute-start(f32[2,192,1024]{2,1,0:T(8,128)S(1)} %get-tuple-element.234), channel_id=1, source_target_pairs={{0,1},{1,2},{2,3},{3,4},{4,5},{5,6},{6,7},{7,0},{8,9},{9,10},{10,1... | collective-permute-start | bytes 4718600 | tf_op jit(solution)/shard_map/ppermute | solution.py:33
where the time goes:
time: 502 us; the launch traced here: 499 us
  waiting for transfers between devices  329 us (66%)
  matrix products  86.9 us (17%)
  starting transfers between devices  43 us (9%)
  other arithmetic  26.8 us (5%)
  local copies, waits for them, and re-layouts  13 us (3%)
    ppermute x6, waiting for transfers between devices, from_behind(): return lax.ppermute(shard, axis, pairs)  206 us
    ppermute x2, waiting for transfers between devices, passed_along(): lax.ppermute(shard, axis, [(i, (i + by) % size) for i in range(size)])  83 us
    ppermute x1, waiting for transfers between devices, padded(): lax.ppermute(lax.slice_in_dim(block, 0, width, axis=dim), axis, backward)  30.1 us
    ppermute x6, starting transfers between devices, from_behind(): return lax.ppermute(shard, axis, pairs)  23.8 us
    dot_general x8, matrix products, head_step(): lax.dot_general(weight_b, g_head, (((0,), (0,)), ((), ())), preferred_ele...  18.8 us
    dot_general x8, matrix products, head_step(): lax.dot_general(dscore, q_head, (((0,), (0,)), ((), ())), preferred_eleme...  17.6 us
    dot_general x8, matrix products, head_step(): lax.dot_general(g_head, v_head, (((1,), (1,)), ((), ())), preferred_eleme...  13.2 us
    dot_general x8, matrix products, head_step(): jnp.dot(weight_b, v_head, preferred_element_type=jnp.float32)  12.8 us
  transfers between devices with their start and end apart: 10, of which 10 were waited for; matrix products, arithmetic and copies ran while one was open for 0% of the time, Pallas kernels for 0%

commit v1 on v0

v1 whole, which is shorter than its diff:
```python
import jax
import jax.numpy as jnp
from jax import lax
from jax.experimental import pallas as pl
from jax.experimental.pallas import tpu as pltpu
from jax.sharding import PartitionSpec as P

HEADS = 8
DIM = 128
HOPS = 4
ROWS = 192
KEYS = 3 * ROWS
QUERIES = HOPS * ROWS
TILE = 256
SCALE = DIM ** (-0.5)
LOG2E = 1.4426950408889634
STAT_FROM = (-3, -2, -1, 1, 2, 3)
MESH = pl.DeviceIdType.MESH
F32 = jnp.float32
BF16 = jnp.bfloat16


def nt_dot(a, b):
    return lax.dot_general(a, b, (((1,), (1,)), ((), ())), preferred_element_type=F32)


def tn_dot(a, b):
    return lax.dot_general(a, b, (((0,), (0,)), ((), ())), preferred_element_type=F32)


def kernel(
    q_in, k_in, v_in, g_in,
    o_out, dq_out, dk_out, dv_out,
    kv, qg, prob, dprob, wb, ds, top, st_send, st_recv,
    own_kv, rk_send, rk_recv, oq, rq_recv,
    load_sem, kv_ss, kv_rs, qg_ss, qg_rs, st_ss, st_rs, rk_ss, rk_rs, rq_ss, rq_rs,
):
    o = lax.axis_index("outer")
    i = lax.axis_index("inner")
    n_outer = lax.axis_size("outer")
    n_inner = lax.axis_size("inner")
    left = lax.rem(i + n_inner - 1, n_inner)
    right = lax.rem(i + 1, n_inner)
    slot = lax.rem(o, HOPS)

    def exists(delta):
        return o + delta >= 0 if delta < 0 else o + delta < n_outer

    def load(n):
        cols = pl.ds(pl.multiple_of(n * DIM, DIM), DIM)
        return (
            pltpu.make_async_copy(k_in.at[:, cols], kv.at[n, 1, 0], load_sem.at[n, 0]),
            pltpu.make_async_copy(v_in.at[:, cols], kv.at[n, 1, 1], load_sem.at[n, 1]),
            pltpu.make_async_copy(q_in.at[:, cols], qg.at[n, slot, 0], load_sem.at[n, 2]),
            pltpu.make_async_copy(g_in.at[:, cols], qg.at[n, slot, 1], load_sem.at[n, 3]),
        )

    @pl.loop(0, HEADS)
    def _(n):
        for copy in load(n):
            copy.start()

    barrier = pltpu.get_barrier_semaphore()
    for other in (left, right):
        pl.semaphore_signal(barrier, inc=1, device_id=(o, other), device_id_type=MESH)
    for delta in STAT_FROM:
        @pl.when(exists(delta))
        def _():
            pl.semaphore_signal(barrier, inc=1, device_id=(o + delta, i), device_id_type=MESH)

    for h in range(1, HOPS):
        @pl.when(jnp.logical_not(exists(h)))
        def _():
            qg[:, lax.rem(o + h, HOPS)] = jnp.zeros((HEADS, 2, ROWS, DIM), BF16)

        @pl.when(jnp.logical_not(exists(-h)))
        def _():
            rq_recv[:, h - 1] = jnp.zeros((HEADS, 2, ROWS, DIM), BF16)
    for at, delta in enumerate(STAT_FROM):
        @pl.when(jnp.logical_not(exists(delta)))
        def _():
            st_recv[:, at] = jnp.zeros((HEADS, 2, QUERIES), F32)

    behind = jnp.minimum(o, HOPS - 1)
    ahead = jnp.minimum(n_outer - 1 - o, HOPS - 1)
    pl.semaphore_wait(barrier, 2 + behind + ahead)

    def kv_copy(n, to):
        return pltpu.make_async_remote_copy(
            kv.at[n, 1], kv.at[n, 2 - 2 * to], kv_ss.at[n, to], kv_rs.at[n, to],
            device_id=(o, (left, right)[to]), device_id_type=MESH,
        )

    def qg_copy(n, h):
        return pltpu.make_async_remote_copy(
            qg.at[n, slot], qg.at[n, slot], qg_ss.at[n, h - 1], qg_rs.at[n, h - 1],
            device_id=(o - h, i), device_id_type=MESH,
        )

    def qg_arrival(n, h):
        at = lax.rem(o + h, HOPS)
        return pltpu.make_async_remote_copy(
            qg.at[n, at], qg.at[n, at], qg_ss.at[n, h - 1], qg_rs.at[n, h - 1],
            device_id=(o, i), device_id_type=MESH,
        )

    def st_copy(n, delta):
        at = STAT_FROM.index(-delta)
        return pltpu.make_async_remote_copy(
            st_send.at[n], st_recv.at[n, at], st_ss.at[n, at], st_rs.at[n, at],
            device_id=(o + delta, i), device_id_type=MESH,
        )

    def rk_copy(n, to):
        return pltpu.make_async_remote_copy(
            rk_send.at[n, to], rk_recv.at[n, to], rk_ss.at[n, to], rk_rs.at[n, to],
            device_id=(o, (left, right)[to]), device_id_type=MESH,
        )

    def rq_copy(n, h):
        return pltpu.make_async_remote_copy(
            oq.at[n, lax.rem(o + h, HOPS)], rq_recv.at[n, h - 1],
            rq_ss.at[n, h - 1], rq_rs.at[n, h - 1],
            device_id=(o + h, i), device_id_type=MESH,
        )

    @pl.loop(0, HEADS)
    def _(n):
        for copy in load(n):
            copy.wait()
        for to in range(2):
            kv_copy(n, to).start()
        for h in range(1, HOPS):
            @pl.when(exists(-h))
            def _():
                qg_copy(n, h).start()

    lane = lax.broadcasted_iota(jnp.int32, (1, QUERIES), 1)
    at_slot = sum((lane >= ROWS * s).astype(jnp.int32) for s in range(1, HOPS))
    hop_of = (at_slot - slot + HOPS) & (HOPS - 1)

    def first(n):
        par = n & 1
        for to in range(2):
            kv_copy(n, to).wait_recv()
        for h in range(1, HOPS):
            @pl.when(exists(h))
            def _():
                qg_arrival(n, h).wait_recv()
        q = qg[n, :, 0].reshape(QUERIES, DIM)
        g = qg[n, :, 1].reshape(QUERIES, DIM)
        tops, sums, dots = [], [], []
        for b in range(3):
            k = kv[n, b, 0]
            v = kv[n, b, 1]
            t_row, s_row, d_row = [], [], []
            for t in range(QUERIES // TILE):
                cols = slice(t * TILE, (t + 1) * TILE)
                s = nt_dot(k, q[cols])
                high = jnp.max(s, axis=0, keepdims=True)
                p = jnp.exp2((s - high) * (SCALE * LOG2E))
                dp = nt_dot(v, g[cols])
                prob[par, b, :, cols] = p
                dprob[par, b, :, cols] = dp
                t_row.append(high * (SCALE * LOG2E))
                s_row.append(jnp.sum(p, axis=0, keepdims=True))
                d_row.append(jnp.sum(p * dp, axis=0, keepdims=True))
            tops.append(jnp.concatenate(t_row, axis=1))
            sums.append(jnp.concatenate(s_row, axis=1))
            dots.append(jnp.concatenate(d_row, axis=1))
            top[par, b] = tops[-1]
        best = jnp.maximum(jnp.maximum(tops[0], tops[1]), tops[2])
        total = jnp.zeros_like(best)
        dot = jnp.zeros_like(best)
        for b in range(3):
            factor = jnp.exp2(tops[b] - best)
            total += factor * sums[b]
            dot += factor * dots[b]
        st_send[n, 0:1, :] = best + jnp.log2(total)
        st_send[n, 1:2, :] = dot / total
        for delta in STAT_FROM:
            @pl.when(exists(delta))
            def _():
                st_copy(n, delta).start()

    def second(n):
        par = n & 1
        for delta in STAT_FROM:
            @pl.when(exists(delta))
            def _():
                st_copy(n, -delta).wait_recv()
        logs = [st_send[n, 0:1, :]]
        dots = [st_send[n, 1:2, :]]
        for at, delta in enumerate(STAT_FROM):
            shared = (hop_of >= delta) if delta > 0 else (hop_of <= HOPS - 1 + delta)
            shared = jnp.logical_and(shared, exists(delta))
            logs.append(jnp.where(shared, st_recv[n, at, 0:1, :], -1e30))
            dots.append(jnp.where(shared, st_recv[n, at, 1:2, :], 0.0))
        best = logs[0]
        for x in logs[1:]:
            best = jnp.maximum(best, x)
        total = jnp.zeros_like(best)
        delta_row = jnp.zeros_like(best)
        for x, d in zip(logs, dots):
            factor = jnp.exp2(x - best)
            total += factor
            delta_row += factor * d
        delta_row = delta_row / total
        log_all = best + jnp.log2(total)
        for b in range(3):
            factor = jnp.exp2(top[par, b] - log_all)
            w = prob[par, b] * factor
            wb[b] = w.astype(BF16)
            ds[b] = (w * (dprob[par, b] - delta_row)).astype(BF16)
        w_all = wb[...].reshape(KEYS, QUERIES)
        s_all = ds[...].reshape(KEYS, QUERIES)
        q = qg[n, :, 0].reshape(QUERIES, DIM)
        g = qg[n, :, 1].reshape(QUERIES, DIM)
        dv = jnp.dot(w_all, g, preferred_element_type=F32)
        dk = jnp.dot(s_all, q, preferred_element_type=F32) * SCALE
        for to, b in ((0, 0), (1, 2)):
            rk_send[n, to, 0] = dk[b * ROWS:(b + 1) * ROWS].astype(BF16)
            rk_send[n, to, 1] = dv[b * ROWS:(b + 1) * ROWS].astype(BF16)
            rk_copy(n, to).start()
        own_kv[n, 0] = dk[ROWS:2 * ROWS]
        own_kv[n, 1] = dv[ROWS:2 * ROWS]
        k_all = kv[n, :, 0].reshape(KEYS, DIM)
        v_all = kv[n, :, 1].reshape(KEYS, DIM)
        out = tn_dot(v_all, w_all).T
        dq = (tn_dot(k_all, s_all) * SCALE).T
        oq[n, :, 0] = out.astype(BF16).reshape(HOPS, ROWS, DIM)
        oq[n, :, 1] = dq.astype(BF16).reshape(HOPS, ROWS, DIM)
        for h in range(HOPS - 1, 0, -1):
            @pl.when(exists(h))
            def _():
                rq_copy(n, h).start()

    first(0)

    @pl.loop(1, HEADS)
    def _(n):
        first(n)
        second(n - 1)

    second(HEADS - 1)

    @pl.loop(0, HEADS)
    def _(n):
        for to in range(2):
            rk_copy(n, to).wait_recv()
        for h in range(1, HOPS):
            @pl.when(exists(-h))
            def _():
                rq_copy(n, h).wait_recv()
        cols = pl.ds(pl.multiple_of(n * DIM, DIM), DIM)
        for part, out in ((0, dk_out), (1, dv_out)):
            total = own_kv[n, part]
            for to in range(2):
                total += rk_recv[n, to, part].astype(F32)
            out[:, cols] = total.astype(BF16)
        for part, out in ((0, o_out), (1, dq_out)):
            total = oq[n, slot, part].astype(F32)
            for h in range(1, HOPS):
                total += rq_recv[n, h - 1, part].astype(F32)
            out[:, cols] = total.astype(BF16)

    @pl.loop(0, HEADS)
    def _(n):
        for to in range(2):
            kv_copy(n, to).wait_send()
            rk_copy(n, to).wait_send()
        for h in range(1, HOPS):
            @pl.when(exists(-h))
            def _():
                qg_copy(n, h).wait_send()

            @pl.when(exists(h))
            def _():
                rq_copy(n, h).wait_send()
        for delta in STAT_FROM:
            @pl.when(exists(delta))
            def _():
                st_copy(n, delta).wait_send()


def on_device(queries, keys, values, d_out):
    block = jax.ShapeDtypeStruct((ROWS, HEADS * DIM), BF16)
    vmem = pl.BlockSpec(memory_space=pltpu.VMEM)
    dma = pltpu.SemaphoreType.DMA
    return pl.pallas_call(
        kernel,
        out_shape=(block,) * 4,
        in_specs=[pl.BlockSpec(memory_space=pl.ANY)] * 4,
        out_specs=(vmem,) * 4,
        scratch_shapes=[
            pltpu.VMEM((HEADS, 3, 2, ROWS, DIM), BF16),
            pltpu.VMEM((HEADS, HOPS, 2, ROWS, DIM), BF16),
            pltpu.VMEM((2, 3, ROWS, QUERIES), F32),
            pltpu.VMEM((2, 3, ROWS, QUERIES), F32),
            pltpu.VMEM((3, ROWS, QUERIES), BF16),
            pltpu.VMEM((3, ROWS, QUERIES), BF16),
            pltpu.VMEM((2, 3, 1, QUERIES), F32),
            pltpu.VMEM((HEADS, 2, QUERIES), F32),
            pltpu.VMEM((HEADS, 6, 2, QUERIES), F32),
            pltpu.VMEM((HEADS, 2, ROWS, DIM), F32),
            pltpu.VMEM((HEADS, 2, 2, ROWS, DIM), BF16),
            pltpu.VMEM((HEADS, 2, 2, ROWS, DIM), BF16),
            pltpu.VMEM((HEADS, HOPS, 2, ROWS, DIM), BF16),
            pltpu.VMEM((HEADS, HOPS - 1, 2, ROWS, DIM), BF16),
            dma((HEADS, 4)),
            dma((HEADS, 2)), dma((HEADS, 2)),
            dma((HEADS, 3)), dma((HEADS, 3)),
            dma((HEADS, 6)), dma((HEADS, 6)),
            dma((HEADS, 2)), dma((HEADS, 2)),
            dma((HEADS, 3)), dma((HEADS, 3)),
        ],
        compiler_params=pltpu.CompilerParams(
            collective_id=0, has_side_effects=True, vmem_limit_bytes=56 << 20
        ),
        cost_estimate=pl.CostEstimate(
            flops=12 * HEADS * KEYS * QUERIES * DIM,
            bytes_accessed=8 * ROWS * HEADS * DIM * 2,
            transcendentals=HEADS * KEYS * QUERIES,
        ),
        name="window_attention",
    )(queries, keys, values, d_out)


def solution(mesh):
    placed = P(("outer", "inner"), None)
    return jax.shard_map(
        on_device,
        mesh=mesh,
        in_specs=(placed,) * 4,
        out_specs=(placed,) * 4,
        check_vma=False,
    )
```

time: 502 us -> 157 us (0.31)
  the two profiles are of different devices: /device:TPU:121 before, /device:TPU:7 now
where the time goes in v1:
time: 157 us; the launch traced here: 156 us
  Pallas kernels  151 us (96%)
  local copies, waits for them, and re-layouts  4.84 us (3%)
    pallas_call x1, Pallas kernels, on_device(): pl.pallas_call(kernel, out_shape=(block,) * 4, in_specs=[pl.BlockSpec(mem...  151 us
    unnamed x10, local copies, waits for them, and re-layouts  4.84 us

profile of v1, /device:TPU:7, one launch (start us, length us, event | category | flops | bytes accessed | tf_op | source)
XLA Modules:
  0.0 156.4 jit_solution(6833757933383297474)
XLA Ops:
  0.6 150.9 %window_attention.1 = (bf16[192,1024]{1,0:T(8,128)(2,1)}, bf16[192,1024]{1,0:T(8,128)(2,1)}, bf16[192,1024]{1,0:T(8,128)(2,1)}, bf16[192,1024]{1,0:T(8,128)(2,1)}) custom-call(bf16[192,1024]{1,0:T(8,128)(2,1)} %q_in.1, bf16[192,1024]{1,0:T(8,128)(2,1)} %k_in.1, bf16[192,1024]{1,0:T(8,128)(2,1)} %v_in.1, bf16[192,1024]{1,0:T(8,128)(2,1)} %g_in.1), custom_call_target="tpu_custom_call" | custom-call | flops 5435817984 | bytes 3145728 | tf_op jit(solution)/shard_map/window_attention/pallas_call | solution.py:290
  151.6 0.0 copy-start.2
  151.6 1.8 %copy.12 = bf16[192,1024]{1,0:T(8,128)(2,1)} copy(bf16[192,1024]{1,0:T(8,128)(2,1)} %get-tuple-element.8) | data formatting | bytes 786432
  153.4 0.0 copy-done.2
  153.4 0.0 copy-start.1
  153.4 0.7 copy.13
  154.1 0.4 copy-done.1
  154.5 0.0 copy-start
  154.5 0.7 copy.14
  155.3 0.4 copy-done
  155.7 0.7 copy.15
Async XLA Ops:
  151.6 1.8 %copy-start.2 = (bf16[192,1024]{1,0:T(8,128)(2,1)S(1)}, bf16[192,1024]{1,0:T(8,128)(2,1)}, u32[]{:S(2)}) copy-start(bf16[192,1024]{1,0:T(8,128)(2,1)} %get-tuple-element.9) | copy-start | bytes 1179652
  153.4 1.1 copy-start.1
  154.5 1.1 copy-start

commit v2 on v1

--- a/solution.py
+++ b/solution.py
@@ -32,8 +32,9 @@
     q_in, k_in, v_in, g_in,
     o_out, dq_out, dk_out, dv_out,
     kv, qg, prob, dprob, wb, ds, top, st_send, st_recv,
-    own_kv, rk_send, rk_recv, oq, rq_recv,
-    load_sem, kv_ss, kv_rs, qg_ss, qg_rs, st_ss, st_rs, rk_ss, rk_rs, rq_ss, rq_rs,
+    own_kv, rk_send, rk_recv, relayed, oq, rq_recv,
+    load_sem, kv_ss, kv_rs, kv_fs, qg_ss, qg_rs, st_ss, st_rs,
+    rk_ss, rk_rs, re_ss, re_rs, rk_fs, rq_ss, rq_rs,
 ):
     o = lax.axis_index("outer")
     i = lax.axis_index("inner")
@@ -42,6 +43,11 @@
     left = lax.rem(i + n_inner - 1, n_inner)
     right = lax.rem(i + 1, n_inner)
     slot = lax.rem(o, HOPS)
+    x = lax.rem(i, 4)
+    first_x, last_x = x == 0, x == 3
+    relays = jnp.logical_or(x == 1, x == 2)
+    up = (x == 2).astype(jnp.int32)
+    far = lax.rem(jnp.where(x >= 2, i + 2, i + n_inner - 2), n_inner)
 
     def exists(delta):
         return o + delta >= 0 if delta < 0 else o + delta < n_outer
@@ -61,7 +67,7 @@
             copy.start()
 
     barrier = pltpu.get_barrier_semaphore()
-    for other in (left, right):
+    for other in (left, right, far):
         pl.semaphore_signal(barrier, inc=1, device_id=(o, other), device_id_type=MESH)
     for delta in STAT_FROM:
         @pl.when(exists(delta))
@@ -72,18 +78,18 @@
         @pl.when(jnp.logical_not(exists(h)))
         def _():
             qg[:, lax.rem(o + h, HOPS)] = jnp.zeros((HEADS, 2, ROWS, DIM), BF16)
-
-        @pl.when(jnp.logical_not(exists(-h)))
-        def _():
-            rq_recv[:, h - 1] = jnp.zeros((HEADS, 2, ROWS, DIM), BF16)
     for at, delta in enumerate(STAT_FROM):
         @pl.when(jnp.logical_not(exists(delta)))
         def _():
             st_recv[:, at] = jnp.zeros((HEADS, 2, QUERIES), F32)
 
+    @pl.when(o == 0)
+    def _():
+        rq_recv[:, 0] = jnp.zeros((HEADS, 2, ROWS, DIM), BF16)
+
     behind = jnp.minimum(o, HOPS - 1)
     ahead = jnp.minimum(n_outer - 1 - o, HOPS - 1)
-    pl.semaphore_wait(barrier, 2 + behind + ahead)
+    pl.semaphore_wait(barrier, 3 + behind + ahead)
 
     def kv_copy(n, to):
         return pltpu.make_async_remote_copy(
@@ -91,18 +97,66 @@
             device_id=(o, (left, right)[to]), device_id_type=MESH,
         )
 
+    def relayed_to(n, to):
+        return jnp.logical_and((first_x, last_x)[to], (n & 1) == 1)
+
+    def kv_send(n):
+        for to in range(2):
+            @pl.when(jnp.logical_not(relayed_to(n, to)))
+            def _():
+                kv_copy(n, to).start()
+
+    def kv_forward_copy(n):
+        return pltpu.make_async_remote_copy(
+            kv.at[n, 2 * up], kv.at[n, 2 - 2 * up], kv_fs.at[n >> 1], kv_rs.at[n, up],
+            device_id=(o, far), device_id_type=MESH,
+        )
+
+    def kv_forward(n):
+        @pl.when(x == 1)
+        def _():
+            kv_copy(n, 1).wait_recv()
+
+        @pl.when(x == 2)
+        def _():
+            kv_copy(n, 0).wait_recv()
+
+        @pl.when(relays)
+        def _():
+            kv_forward_copy(n).start()
+
+    def kv_wait(n):
+        odd = (n & 1) == 1
+        for to in range(2):
+            @pl.when(jnp.logical_not(jnp.logical_and(x == 2 - to, odd)))
+            def _():
+                kv_copy(n, to).wait_recv()
+
     def qg_copy(n, h):
-        return pltpu.make_async_remote_copy(
-            qg.at[n, slot], qg.at[n, slot], qg_ss.at[n, h - 1], qg_rs.at[n, h - 1],
-            device_id=(o - h, i), device_id_type=MESH,
-        )
-
-    def qg_arrival(n, h):
         at = lax.rem(o + h, HOPS)
         return pltpu.make_async_remote_copy(
-            qg.at[n, at], qg.at[n, at], qg_ss.at[n, h - 1], qg_rs.at[n, h - 1],
-            device_id=(o, i), device_id_type=MESH,
-        )
+            qg.at[n, at], qg.at[n, at], qg_ss.at[n, h], qg_rs.at[n, h],
+            device_id=(o - 1, i), device_id_type=MESH,
+        )
+
+    def qg_send(n, h):
+        @pl.when(jnp.logical_and(o > 0, exists(h)))
+        def _():
+            qg_copy(n, h).start()
+
+    def qg_wait(n, h):
+        at = lax.rem(o + h, HOPS)
+
+        @pl.when(exists(h))
+        def _():
+            pltpu.make_async_remote_copy(
+                qg.at[n, at], qg.at[n, at], qg_ss.at[n, h - 1], qg_rs.at[n, h - 1],
+                device_id=(o - 1, i), device_id_type=MESH,
+            ).wait_recv()
+
+    def qg_forward(n, h):
+        qg_wait(n, h)
+        qg_send(n, h)
 
     def st_copy(n, delta):
         at = STAT_FROM.index(-delta)
@@ -117,23 +171,67 @@
             device_id=(o, (left, right)[to]), device_id_type=MESH,
         )
 
+    def relay_copy(n, to):
+        return pltpu.make_async_remote_copy(
+            rk_send.at[n, to], relayed.at[n >> 1], re_ss.at[n >> 1], re_rs.at[n >> 1],
+            device_id=(o, (right, left)[to]), device_id_type=MESH,
+        )
+
+    def rk_start(n):
+        for to in range(2):
+            @pl.when(jnp.logical_not(relayed_to(n, to)))
+            def _():
+                rk_copy(n, to).start()
+
+            @pl.when(relayed_to(n, to))
+            def _():
+                relay_copy(n, to).start()
+
+    def rk_forward_copy(n):
+        return pltpu.make_async_remote_copy(
+            relayed.at[n >> 1], rk_recv.at[n, up], rk_fs.at[n >> 1], rk_rs.at[n, up],
+            device_id=(o, far), device_id_type=MESH,
+        )
+
+    def rk_forward(n):
+        @pl.when(relays)
+        def _():
+            relay_copy(n, 0).wait_recv()
+            rk_forward_copy(n).start()
+
     def rq_copy(n, h):
         return pltpu.make_async_remote_copy(
             oq.at[n, lax.rem(o + h, HOPS)], rq_recv.at[n, h - 1],
             rq_ss.at[n, h - 1], rq_rs.at[n, h - 1],
-            device_id=(o + h, i), device_id_type=MESH,
-        )
-
-    @pl.loop(0, HEADS)
-    def _(n):
+            device_id=(o + 1, i), device_id_type=MESH,
+        )
+
+    def rq_send(n, h):
+        @pl.when(exists(h))
+        def _():
+            rq_copy(n, h).start()
+
+    def rq_wait(n, h):
+        pltpu.make_async_remote_copy(
+            oq.at[n, 0], rq_recv.at[n, h], rq_ss.at[n, h], rq_rs.at[n, h],
+            device_id=(o + 1, i), device_id_type=MESH,
+        ).wait_recv()
+
+    def rq_pass(n, h):
+        at = lax.rem(o + h, HOPS)
+
+        @pl.when(jnp.logical_and(o > 0, exists(h)))
+        def _():
+            rq_wait(n, h)
+            oq[n, at] = (oq[n, at].astype(F32) + rq_recv[n, h].astype(F32)).astype(BF16)
+
+        rq_send(n, h)
+
+    for n in range(HEADS):
         for copy in load(n):
             copy.wait()
-        for to in range(2):
-            kv_copy(n, to).start()
-        for h in range(1, HOPS):
-            @pl.when(exists(-h))
-            def _():
-                qg_copy(n, h).start()
+        kv_send(n)
+        qg_send(n, 0)
 
     lane = lax.broadcasted_iota(jnp.int32, (1, QUERIES), 1)
     at_slot = sum((lane >= ROWS * s).astype(jnp.int32) for s in range(1, HOPS))
@@ -141,12 +239,8 @@
 
     def first(n):
         par = n & 1
-        for to in range(2):
-            kv_copy(n, to).wait_recv()
-        for h in range(1, HOPS):
-            @pl.when(exists(h))
-            def _():
-                qg_arrival(n, h).wait_recv()
+        kv_wait(n)
+        qg_wait(n, 3)
         q = qg[n, :, 0].reshape(QUERIES, DIM)
         g = qg[n, :, 1].reshape(QUERIES, DIM)
         tops, sums, dots = [], [], []
@@ -221,7 +315,7 @@
         for to, b in ((0, 0), (1, 2)):
             rk_send[n, to, 0] = dk[b * ROWS:(b + 1) * ROWS].astype(BF16)
             rk_send[n, to, 1] = dv[b * ROWS:(b + 1) * ROWS].astype(BF16)
-            rk_copy(n, to).start()
+        rk_start(n)
         own_kv[n, 0] = dk[ROWS:2 * ROWS]
         own_kv[n, 1] = dv[ROWS:2 * ROWS]
         k_all = kv[n, :, 0].reshape(KEYS, DIM)
@@ -230,28 +324,53 @@
         dq = (tn_dot(k_all, s_all) * SCALE).T
         oq[n, :, 0] = out.astype(BF16).reshape(HOPS, ROWS, DIM)
         oq[n, :, 1] = dq.astype(BF16).reshape(HOPS, ROWS, DIM)
-        for h in range(HOPS - 1, 0, -1):
-            @pl.when(exists(h))
-            def _():
-                rq_copy(n, h).start()
-
+        rq_send(n, 3)
+
+    def when_head(n, do, *rest):
+        @pl.when(jnp.logical_and(n >= 0, n < HEADS))
+        def _():
+            do(n, *rest)
+
+    def ahead_of(t):
+        when_head(2 * t + 1, kv_forward)
+        when_head(t + 2, qg_forward, 1)
+        when_head(t + 1, qg_forward, 2)
+
+    qg_forward(0, 1)
+    qg_forward(1, 1)
+    qg_forward(0, 2)
+    ahead_of(0)
     first(0)
 
     @pl.loop(1, HEADS)
-    def _(n):
-        first(n)
-        second(n - 1)
+    def _(t):
+        ahead_of(t)
+        first(t)
+        second(t - 1)
+        when_head(t - 2, rq_pass, 2)
+        when_head(t - 3, rq_pass, 1)
+
+        @pl.when(jnp.logical_and(t >= 3, (t & 1) == 1))
+        def _():
+            rk_forward(t - 2)
 
     second(HEADS - 1)
+    rq_pass(HEADS - 2, 2)
+    rq_pass(HEADS - 3, 1)
+    rq_pass(HEADS - 1, 2)
+    rq_pass(HEADS - 2, 1)
+    rq_pass(HEADS - 1, 1)
+    rk_forward(HEADS - 1)
 
     @pl.loop(0, HEADS)
     def _(n):
         for to in range(2):
             rk_copy(n, to).wait_recv()
-        for h in range(1, HOPS):
-            @pl.when(exists(-h))
-            def _():
-                rq_copy(n, h).wait_recv()
+
+        @pl.when(o > 0)
+        def _():
+            rq_wait(n, 0)
+
         cols = pl.ds(pl.multiple_of(n * DIM, DIM), DIM)
         for part, out in ((0, dk_out), (1, dv_out)):
             total = own_kv[n, part]
@@ -259,35 +378,49 @@
                 total += rk_recv[n, to, part].astype(F32)
             out[:, cols] = total.astype(BF16)
         for part, out in ((0, o_out), (1, dq_out)):
-            total = oq[n, slot, part].astype(F32)
-            for h in range(1, HOPS):
-                total += rq_recv[n, h - 1, part].astype(F32)
-            out[:, cols] = total.astype(BF16)
+            out[:, cols] = (oq[n, slot, part].astype(F32) + rq_recv[n, 0, part].astype(F32)).astype(BF16)
 
     @pl.loop(0, HEADS)
     def _(n):
         for to in range(2):
-            kv_copy(n, to).wait_send()
-            rk_copy(n, to).wait_send()
-        for h in range(1, HOPS):
-            @pl.when(exists(-h))
+            @pl.when(jnp.logical_not(relayed_to(n, to)))
+            def _():
+                kv_copy(n, to).wait_send()
+                rk_copy(n, to).wait_send()
+
+            @pl.when(relayed_to(n, to))
+            def _():
+                relay_copy(n, to).wait_send()
+
+        @pl.when(jnp.logical_and(relays, (n & 1) == 1))
+        def _():
+            kv_forward_copy(n).wait_send()
+            rk_forward_copy(n).wait_send()
+
+        for h in range(HOPS - 1):
+            @pl.when(jnp.logical_and(o > 0, exists(h)))
             def _():
                 qg_copy(n, h).wait_send()
 
-            @pl.when(exists(h))
-            def _():
-                rq_copy(n, h).wait_send()
+            @pl.when(exists(h + 1))
+            def _():
+                rq_copy(n, h + 1).wait_send()
         for delta in STAT_FROM:
             @pl.when(exists(delta))
             def _():
                 st_copy(n, delta).wait_send()
+
+
+def store(*refs):
+    for a, b in zip(refs[:4], refs[4:]):
+        b[...] = a[...]
 
 
 def on_device(queries, keys, values, d_out):
     block = jax.ShapeDtypeStruct((ROWS, HEADS * DIM), BF16)
     vmem = pl.BlockSpec(memory_space=pltpu.VMEM)
     dma = pltpu.SemaphoreType.DMA
-    return pl.pallas_call(
+    results = pl.pallas_call(
         kernel,
         out_shape=(block,) * 4,
         in_specs=[pl.BlockSpec(memory_space=pl.ANY)] * 4,
@@ -305,13 +438,15 @@
             pltpu.VMEM((HEADS, 2, ROWS, DIM), F32),
             pltpu.VMEM((HEADS, 2, 2, ROWS, DIM), BF16),
             pltpu.VMEM((HEADS, 2, 2, ROWS, DIM), BF16),
+            pltpu.VMEM((HEADS // 2, 2, ROWS, DIM), BF16),
             pltpu.VMEM((HEADS, HOPS, 2, ROWS, DIM), BF16),
             pltpu.VMEM((HEADS, HOPS - 1, 2, ROWS, DIM), BF16),
             dma((HEADS, 4)),
-            dma((HEADS, 2)), dma((HEADS, 2)),
+            dma((HEADS, 2)), dma((HEADS, 2)), dma((HEADS // 2,)),
             dma((HEADS, 3)), dma((HEADS, 3)),
             dma((HEADS, 6)), dma((HEADS, 6)),
             dma((HEADS, 2)), dma((HEADS, 2)),
+            dma((HEADS // 2,)), dma((HEADS // 2,)), dma((HEADS // 2,)),
             dma((HEADS, 3)), dma((HEADS, 3)),
         ],
         compiler_params=pltpu.CompilerParams(
@@ -324,6 +459,13 @@
         ),
         name="window_attention",
     )(queries, keys, values, d_out)
+    return pl.pallas_call(
+        store,
+        out_shape=(block,) * 4,
+        in_specs=[vmem] * 4,
+        out_specs=(vmem,) * 4,
+        name="store_results",
+    )(*results)
 
 
 def solution(mesh):

time: 157 us -> 110 us (0.70)
  the two profiles are of different devices: /device:TPU:7 before, /device:TPU:128 now
where the time goes in v2:
time: 110 us
  Pallas kernels  109 us (99%)
    pallas_call x1, Pallas kernels, on_device(): pl.pallas_call(kernel, out_shape=(block,) * 4, in_specs=[pl.BlockSpec(mem...  107 us
    pallas_call x1, Pallas kernels, on_device(): pl.pallas_call(store, out_shape=(block,) * 4, in_specs=[vmem] * 4, out_sp...  2.51 us

profile of v2, /device:TPU:128, one launch (start us, length us, event | category | flops | bytes accessed | tf_op | source)
XLA Modules:
  0.0 109.7 jit_solution(3069172928516485181)
XLA Ops:
  0.6 106.5 %window_attention.1 = (bf16[192,1024]{1,0:T(8,128)(2,1)}, bf16[192,1024]{1,0:T(8,128)(2,1)}, bf16[192,1024]{1,0:T(8,128)(2,1)}, bf16[192,1024]{1,0:T(8,128)(2,1)}) custom-call(bf16[192,1024]{1,0:T(8,128)(2,1)} %q_in.1, bf16[192,1024]{1,0:T(8,128)(2,1)} %k_in.1, bf16[192,1024]{1,0:T(8,128)(2,1)} %v_in.1, bf16[192,1024]{1,0:T(8,128)(2,1)} %g_in.1), custom_call_target="tpu_custom_call" | custom-call | flops 5435817984 | bytes 3145728 | tf_op jit(solution)/shard_map/window_attention/pallas_call | solution.py:423
  107.2 2.5 %store_results.1 = (bf16[192,1024]{1,0:T(8,128)(2,1)}, bf16[192,1024]{1,0:T(8,128)(2,1)}, bf16[192,1024]{1,0:T(8,128)(2,1)}, bf16[192,1024]{1,0:T(8,128)(2,1)}) custom-call(bf16[192,1024]{1,0:T(8,128)(2,1)} %get-tuple-element.8.refs_0_, bf16[192,1024]{1,0:T(8,128)(2,1)} %get-tuple-element.9.refs_1_, bf16[192,1024]{1,0:T(8,128)(2,1)} %get-tuple-element.10.refs_2_, ...), custom_call_target="tpu_custom_call" | custom-call | tf_op jit(solution)/shard_map/store_results/pallas_call | solution.py:462

commit v3 on v2

--- a/solution.py
+++ b/solution.py
@@ -14,6 +14,8 @@
 TILE = 256
 SCALE = DIM ** (-0.5)
 LOG2E = 1.4426950408889634
+RUN = 16
+LAG = 2
 STAT_FROM = (-3, -2, -1, 1, 2, 3)
 MESH = pl.DeviceIdType.MESH
 F32 = jnp.float32
@@ -32,9 +34,9 @@
     q_in, k_in, v_in, g_in,
     o_out, dq_out, dk_out, dv_out,
     kv, qg, prob, dprob, wb, ds, top, st_send, st_recv,
-    own_kv, rk_send, rk_recv, relayed, oq, rq_recv,
-    load_sem, kv_ss, kv_rs, kv_fs, qg_ss, qg_rs, st_ss, st_rs,
-    rk_ss, rk_rs, re_ss, re_rs, rk_fs, rq_ss, rq_rs,
+    own_kv, rk_send, rk_recv, relayed, oq, rq_recv, q_held, r_held,
+    load_sem, kv_ss, kv_rs, kv_fs, qg_ss, qg_rs, qg_xs, ql_rs, ql_fs, st_ss, st_rs,
+    rk_ss, rk_rs, re_ss, re_rs, rk_fs, rq_ss, rq_rs, rl_rs, rl_fs,
 ):
     o = lax.axis_index("outer")
     i = lax.axis_index("inner")
@@ -43,6 +45,10 @@
     left = lax.rem(i + n_inner - 1, n_inner)
     right = lax.rem(i + 1, n_inner)
     slot = lax.rem(o, HOPS)
+    place = lax.rem(o, RUN)
+    early, last = place <= HOPS - 2, place == RUN - 1
+    run_before, run_after = o >= RUN, o < n_outer - RUN
+    ends = jnp.logical_or(early, last)
     x = lax.rem(i, 4)
     first_x, last_x = x == 0, x == 3
     relays = jnp.logical_or(x == 1, x == 2)
@@ -74,6 +80,23 @@
         def _():
             pl.semaphore_signal(barrier, inc=1, device_id=(o + delta, i), device_id_type=MESH)
 
+    @pl.when(jnp.logical_and(ends, run_before))
+    def _():
+        pl.semaphore_signal(barrier, inc=1, device_id=(o - RUN, i), device_id_type=MESH)
+
+    @pl.when(jnp.logical_and(ends, run_after))
+    def _():
+        pl.semaphore_signal(barrier, inc=1, device_id=(o + RUN, i), device_id_type=MESH)
+
+    @pl.when(early)
+    def _():
+        pl.semaphore_signal(barrier, inc=1, device_id=(o + RUN - 1 - place, i), device_id_type=MESH)
+
+    @pl.when(last)
+    def _():
+        for p in range(HOPS - 1):
+            pl.semaphore_signal(barrier, inc=1, device_id=(o - RUN + 1 + p, i), device_id_type=MESH)
+
     for h in range(1, HOPS):
         @pl.when(jnp.logical_not(exists(h)))
         def _():
@@ -89,7 +112,9 @@
 
     behind = jnp.minimum(o, HOPS - 1)
     ahead = jnp.minimum(n_outer - 1 - o, HOPS - 1)
-    pl.semaphore_wait(barrier, 3 + behind + ahead)
+    across = run_before.astype(jnp.int32) + run_after.astype(jnp.int32)
+    more = jnp.where(early, 1 + across, jnp.where(last, HOPS - 1 + across, 0))
+    pl.semaphore_wait(barrier, 3 + behind + ahead + more)
 
     def kv_copy(n, to):
         return pltpu.make_async_remote_copy(
@@ -139,10 +164,62 @@
             device_id=(o - 1, i), device_id_type=MESH,
         )
 
+    def qg_turns(n):
+        return jnp.logical_or(place == 2, jnp.logical_and(place < 2, (n & 1) == 1))
+
+    def qg_relayed(n):
+        return jnp.logical_and(run_before, qg_turns(n))
+
+    def qg_sends(n, h):
+        here = jnp.logical_and(o > 0, exists(h))
+        if h == 0:
+            return jnp.logical_and(here, jnp.logical_not(jnp.logical_and(place == 0, qg_relayed(n))))
+        return jnp.logical_and(here, place > 0)
+
+    def qg_cross_copy(n, h):
+        return pltpu.make_async_remote_copy(
+            qg.at[n, slot], qg.at[n, slot], qg_xs.at[n], qg_rs.at[n, h - 1],
+            device_id=(o - h, i), device_id_type=MESH,
+        )
+
+    def qg_crosses(n, h):
+        here = jnp.logical_and(run_before, place == h - 1)
+        return jnp.logical_and(here, jnp.logical_not(qg_turns(n)))
+
+    def qg_relay_copy(n):
+        return pltpu.make_async_remote_copy(
+            qg.at[n, slot], q_held.at[n], qg_xs.at[n], ql_rs.at[n],
+            device_id=(o - RUN, i), device_id_type=MESH,
+        )
+
+    def qg_pass_copy(n):
+        return pltpu.make_async_remote_copy(
+            q_held.at[n], qg.at[n, slot], ql_fs.at[n], qg_rs.at[n, place],
+            device_id=(o + RUN - 1 - place, i), device_id_type=MESH,
+        )
+
+    def qg_passes(n):
+        return jnp.logical_and(run_after, qg_turns(n))
+
+    def qg_pass(n):
+        @pl.when(qg_passes(n))
+        def _():
+            qg_relay_copy(n).wait_recv()
+            qg_pass_copy(n).start()
+
     def qg_send(n, h):
-        @pl.when(jnp.logical_and(o > 0, exists(h)))
+        @pl.when(qg_sends(n, h))
         def _():
             qg_copy(n, h).start()
+
+        if h == 0:
+            @pl.when(qg_crosses(n, 2))
+            def _():
+                qg_cross_copy(n, 2).start()
+
+            @pl.when(qg_relayed(n))
+            def _():
+                qg_relay_copy(n).start()
 
     def qg_wait(n, h):
         at = lax.rem(o + h, HOPS)
@@ -206,8 +283,37 @@
             device_id=(o + 1, i), device_id_type=MESH,
         )
 
+    def rq_relay_copy(n, h):
+        return pltpu.make_async_remote_copy(
+            oq.at[n, lax.rem(o + h, HOPS)], r_held.at[n >> 1, h - 1],
+            rq_ss.at[n, h - 1], rl_rs.at[n >> 1, h - 1],
+            device_id=(o + RUN, i), device_id_type=MESH,
+        )
+
+    def rq_over_copy(n, h):
+        return pltpu.make_async_remote_copy(
+            r_held.at[n >> 1, h - 1], rq_recv.at[n, h - 1],
+            rl_fs.at[n >> 1, h - 1], rq_rs.at[n, h - 1],
+            device_id=(o - RUN + 1, i), device_id_type=MESH,
+        )
+
+    rq_passes = jnp.logical_and(last, run_before)
+
+    def rq_over(n, h):
+        @pl.when(rq_passes)
+        def _():
+            rq_relay_copy(n, h).wait_recv()
+            rq_over_copy(n, h).start()
+
+    def rq_relayed(n):
+        return jnp.logical_and(last, (n & 1) == 1)
+
     def rq_send(n, h):
-        @pl.when(exists(h))
+        @pl.when(jnp.logical_and(exists(h), rq_relayed(n)))
+        def _():
+            rq_relay_copy(n, h).start()
+
+        @pl.when(jnp.logical_and(exists(h), jnp.logical_not(rq_relayed(n))))
         def _():
             rq_copy(n, h).start()
 
@@ -230,15 +336,16 @@
     for n in range(HEADS):
         for copy in load(n):
             copy.wait()
-        kv_send(n)
-        qg_send(n, 0)
+        if n < 4:
+            kv_send(n)
+            qg_send(n, 0)
 
     lane = lax.broadcasted_iota(jnp.int32, (1, QUERIES), 1)
     at_slot = sum((lane >= ROWS * s).astype(jnp.int32) for s in range(1, HOPS))
     hop_of = (at_slot - slot + HOPS) & (HOPS - 1)
 
     def first(n):
-        par = n & 1
+        par = lax.rem(n, LAG + 1)
         kv_wait(n)
         qg_wait(n, 3)
         q = qg[n, :, 0].reshape(QUERIES, DIM)
@@ -278,7 +385,7 @@
                 st_copy(n, delta).start()
 
     def second(n):
-        par = n & 1
+        par = lax.rem(n, LAG + 1)
         for delta in STAT_FROM:
             @pl.when(exists(delta))
             def _():
@@ -331,36 +438,36 @@
         def _():
             do(n, *rest)
 
-    def ahead_of(t):
+    for n in range(2):
+        qg_pass(n)
+    for n in range(3):
+        qg_forward(n, 1)
+    for n in range(2):
+        qg_forward(n, 2)
+
+    @pl.loop(0, HEADS + 7)
+    def _(t):
+        for n in (2 * t + 4, 2 * t + 5):
+            when_head(n, kv_send)
+            when_head(n, qg_send, 0)
+        for n in (2 * t + 2, 2 * t + 3):
+            when_head(n, qg_pass)
         when_head(2 * t + 1, kv_forward)
-        when_head(t + 2, qg_forward, 1)
-        when_head(t + 1, qg_forward, 2)
-
-    qg_forward(0, 1)
-    qg_forward(1, 1)
-    qg_forward(0, 2)
-    ahead_of(0)
-    first(0)
-
-    @pl.loop(1, HEADS)
-    def _(t):
-        ahead_of(t)
-        first(t)
-        second(t - 1)
-        when_head(t - 2, rq_pass, 2)
-        when_head(t - 3, rq_pass, 1)
-
-        @pl.when(jnp.logical_and(t >= 3, (t & 1) == 1))
-        def _():
-            rk_forward(t - 2)
-
-    second(HEADS - 1)
-    rq_pass(HEADS - 2, 2)
-    rq_pass(HEADS - 3, 1)
-    rq_pass(HEADS - 1, 2)
-    rq_pass(HEADS - 2, 1)
-    rq_pass(HEADS - 1, 1)
-    rk_forward(HEADS - 1)
+        when_head(t + 3, qg_forward, 1)
+        when_head(t + 2, qg_forward, 2)
+        when_head(t, first)
+        when_head(t - LAG, second)
+        for h, late in ((3, 3), (2, 5), (1, 7)):
+            @pl.when((t - late) & 1 == 1)
+            def _():
+                when_head(t - late, rq_over, h)
+
+        when_head(t - 4, rq_pass, 2)
+        when_head(t - 6, rq_pass, 1)
+
+        @pl.when((t & 1) == 1)
+        def _():
+            when_head(t - 4, rk_forward)
 
     @pl.loop(0, HEADS)
     def _(n):
@@ -398,13 +505,30 @@
             rk_forward_copy(n).wait_send()
 
         for h in range(HOPS - 1):
-            @pl.when(jnp.logical_and(o > 0, exists(h)))
+            @pl.when(qg_sends(n, h))
             def _():
                 qg_copy(n, h).wait_send()
 
             @pl.when(exists(h + 1))
             def _():
                 rq_copy(n, h + 1).wait_send()
+        @pl.when(qg_crosses(n, 2))
+        def _():
+            qg_cross_copy(n, 2).wait_send()
+
+        @pl.when(qg_relayed(n))
+        def _():
+            qg_relay_copy(n).wait_send()
+
+        @pl.when(qg_passes(n))
+        def _():
+            qg_pass_copy(n).wait_send()
+
+        @pl.when(jnp.logical_and(rq_passes, (n & 1) == 1))
+        def _():
+            for h in range(1, HOPS):
+                rq_over_copy(n, h).wait_send()
+
         for delta in STAT_FROM:
             @pl.when(exists(delta))
             def _():
@@ -428,11 +552,11 @@
         scratch_shapes=[
             pltpu.VMEM((HEADS, 3, 2, ROWS, DIM), BF16),
             pltpu.VMEM((HEADS, HOPS, 2, ROWS, DIM), BF16),
-            pltpu.VMEM((2, 3, ROWS, QUERIES), F32),
-            pltpu.VMEM((2, 3, ROWS, QUERIES), F32),
+            pltpu.VMEM((LAG + 1, 3, ROWS, QUERIES), F32),
+            pltpu.VMEM((LAG + 1, 3, ROWS, QUERIES), F32),
             pltpu.VMEM((3, ROWS, QUERIES), BF16),
             pltpu.VMEM((3, ROWS, QUERIES), BF16),
-            pltpu.VMEM((2, 3, 1, QUERIES), F32),
+            pltpu.VMEM((LAG + 1, 3, 1, QUERIES), F32),
             pltpu.VMEM((HEADS, 2, QUERIES), F32),
             pltpu.VMEM((HEADS, 6, 2, QUERIES), F32),
             pltpu.VMEM((HEADS, 2, ROWS, DIM), F32),
@@ -441,13 +565,16 @@
             pltpu.VMEM((HEADS // 2, 2, ROWS, DIM), BF16),
             pltpu.VMEM((HEADS, HOPS, 2, ROWS, DIM), BF16),
             pltpu.VMEM((HEADS, HOPS - 1, 2, ROWS, DIM), BF16),
+            pltpu.VMEM((HEADS, 2, ROWS, DIM), BF16),
+            pltpu.VMEM((HEADS // 2, HOPS - 1, 2, ROWS, DIM), BF16),
             dma((HEADS, 4)),
             dma((HEADS, 2)), dma((HEADS, 2)), dma((HEADS // 2,)),
-            dma((HEADS, 3)), dma((HEADS, 3)),
+            dma((HEADS, 3)), dma((HEADS, 3)), dma((HEADS,)), dma((HEADS,)), dma((HEADS,)),
             dma((HEADS, 6)), dma((HEADS, 6)),
             dma((HEADS, 2)), dma((HEADS, 2)),
             dma((HEADS // 2,)), dma((HEADS // 2,)), dma((HEADS // 2,)),
             dma((HEADS, 3)), dma((HEADS, 3)),
+            dma((HEADS // 2, 3)), dma((HEADS // 2, 3)),
         ],
         compiler_params=pltpu.CompilerParams(
             collective_id=0, has_side_effects=True, vmem_limit_bytes=56 << 20

time: 110 us -> 97.5 us (0.89)
  the two profiles are of different devices: /device:TPU:128 before, /device:TPU:1 now
where the time goes in v3:
time: 97.5 us; the launch traced here: 97.2 us
  Pallas kernels  96.6 us (99%)
    pallas_call x1, Pallas kernels, on_device(): pl.pallas_call(kernel, out_shape=(block,) * 4, in_specs=[pl.BlockSpec(mem...  94.1 us
    pallas_call x1, Pallas kernels, on_device(): pl.pallas_call(store, out_shape=(block,) * 4, in_specs=[vmem] * 4, out_sp...  2.51 us

profile of v3, /device:TPU:1, one launch (start us, length us, event | category | flops | bytes accessed | tf_op | source)
XLA Modules:
  0.0 97.2 jit_solution(12057282531884366184)
XLA Ops:
  0.6 94.1 %window_attention.1 = (bf16[192,1024]{1,0:T(8,128)(2,1)}, bf16[192,1024]{1,0:T(8,128)(2,1)}, bf16[192,1024]{1,0:T(8,128)(2,1)}, bf16[192,1024]{1,0:T(8,128)(2,1)}) custom-call(bf16[192,1024]{1,0:T(8,128)(2,1)} %q_in.1, bf16[192,1024]{1,0:T(8,128)(2,1)} %k_in.1, bf16[192,1024]{1,0:T(8,128)(2,1)} %v_in.1, bf16[192,1024]{1,0:T(8,128)(2,1)} %g_in.1), custom_call_target="tpu_custom_call" | custom-call | flops 5435817984 | bytes 3145728 | tf_op jit(solution)/shard_map/window_attention/pallas_call | solution.py:547
  94.7 2.5 %store_results.1 = (bf16[192,1024]{1,0:T(8,128)(2,1)}, bf16[192,1024]{1,0:T(8,128)(2,1)}, bf16[192,1024]{1,0:T(8,128)(2,1)}, bf16[192,1024]{1,0:T(8,128)(2,1)}) custom-call(bf16[192,1024]{1,0:T(8,128)(2,1)} %get-tuple-element.8.refs_0_, bf16[192,1024]{1,0:T(8,128)(2,1)} %get-tuple-element.9.refs_1_, bf16[192,1024]{1,0:T(8,128)(2,1)} %get-tuple-element.10.refs_2_, ...), custom_call_target="tpu_custom_call" | custom-call | tf_op jit(solution)/shard_map/store_results/pallas_call | solution.py:589

commit v4 on v3

--- a/solution.py
+++ b/solution.py
@@ -15,11 +15,20 @@
 SCALE = DIM ** (-0.5)
 LOG2E = 1.4426950408889634
 RUN = 16
-LAG = 2
+LAG = 1
+TURN_RING = (1, 3, 5, 6)
+TURN_RUN = (1, 3, 5, 6)
 STAT_FROM = (-3, -2, -1, 1, 2, 3)
 MESH = pl.DeviceIdType.MESH
 F32 = jnp.float32
 BF16 = jnp.bfloat16
+
+
+def among(n, heads):
+    found = n == heads[0]
+    for head in heads[1:]:
+        found = jnp.logical_or(found, n == head)
+    return found
 
 
 def nt_dot(a, b):
@@ -123,7 +132,7 @@
         )
 
     def relayed_to(n, to):
-        return jnp.logical_and((first_x, last_x)[to], (n & 1) == 1)
+        return jnp.logical_and((first_x, last_x)[to], among(n, TURN_RING))
 
     def kv_send(n):
         for to in range(2):
@@ -151,7 +160,7 @@
             kv_forward_copy(n).start()
 
     def kv_wait(n):
-        odd = (n & 1) == 1
+        odd = among(n, TURN_RING)
         for to in range(2):
             @pl.when(jnp.logical_not(jnp.logical_and(x == 2 - to, odd)))
             def _():
@@ -165,7 +174,7 @@
         )
 
     def qg_turns(n):
-        return jnp.logical_or(place == 2, jnp.logical_and(place < 2, (n & 1) == 1))
+        return jnp.logical_or(place == 2, jnp.logical_and(place < 2, among(n, TURN_RUN)))
 
     def qg_relayed(n):
         return jnp.logical_and(run_before, qg_turns(n))
@@ -306,7 +315,7 @@
             rq_over_copy(n, h).start()
 
     def rq_relayed(n):
-        return jnp.logical_and(last, (n & 1) == 1)
+        return jnp.logical_and(last, among(n, TURN_RUN))
 
     def rq_send(n, h):
         @pl.when(jnp.logical_and(exists(h), rq_relayed(n)))
@@ -445,29 +454,33 @@
     for n in range(2):
         qg_forward(n, 2)
 
-    @pl.loop(0, HEADS + 7)
+    @pl.loop(0, HEADS + 6)
     def _(t):
         for n in (2 * t + 4, 2 * t + 5):
             when_head(n, kv_send)
             when_head(n, qg_send, 0)
         for n in (2 * t + 2, 2 * t + 3):
             when_head(n, qg_pass)
-        when_head(2 * t + 1, kv_forward)
+        for n in (2 * t, 2 * t + 1):
+            @pl.when(among(n, TURN_RING))
+            def _():
+                kv_forward(n)
+
         when_head(t + 3, qg_forward, 1)
         when_head(t + 2, qg_forward, 2)
+        @pl.when(among(t - 3, TURN_RING))
+        def _():
+            rk_forward(t - 3)
+
         when_head(t, first)
         when_head(t - LAG, second)
-        for h, late in ((3, 3), (2, 5), (1, 7)):
-            @pl.when((t - late) & 1 == 1)
-            def _():
-                when_head(t - late, rq_over, h)
-
-        when_head(t - 4, rq_pass, 2)
-        when_head(t - 6, rq_pass, 1)
-
-        @pl.when((t & 1) == 1)
-        def _():
-            when_head(t - 4, rk_forward)
+        for h, late in ((3, 2), (2, 4), (1, 6)):
+            @pl.when(among(t - late, TURN_RUN))
+            def _():
+                rq_over(t - late, h)
+
+        when_head(t - 3, rq_pass, 2)
+        when_head(t - 5, rq_pass, 1)
 
     @pl.loop(0, HEADS)
     def _(n):
@@ -499,7 +512,7 @@
             def _():
                 relay_copy(n, to).wait_send()
 
-        @pl.when(jnp.logical_and(relays, (n & 1) == 1))
+        @pl.when(jnp.logical_and(relays, among(n, TURN_RING)))
         def _():
             kv_forward_copy(n).wait_send()
             rk_forward_copy(n).wait_send()
@@ -524,7 +537,7 @@
         def _():
             qg_pass_copy(n).wait_send()
 
-        @pl.when(jnp.logical_and(rq_passes, (n & 1) == 1))
+        @pl.when(jnp.logical_and(rq_passes, among(n, TURN_RUN)))
         def _():
             for h in range(1, HOPS):
                 rq_over_copy(n, h).wait_send()

time: 97.5 us -> 94.6 us (0.970)
  the two profiles are of different devices: /device:TPU:1 before, /device:TPU:196 now
where the time goes in v4:
time: 94.6 us; the launch traced here: 94.4 us
  Pallas kernels  93.8 us (99%)
    pallas_call x1, Pallas kernels, on_device(): pl.pallas_call(kernel, out_shape=(block,) * 4, in_specs=[pl.BlockSpec(mem...  91.3 us
    pallas_call x1, Pallas kernels, on_device(): pl.pallas_call(store, out_shape=(block,) * 4, in_specs=[vmem] * 4, out_sp...  2.51 us

profile of v4, /device:TPU:196, one launch (start us, length us, event | category | flops | bytes accessed | tf_op | source)
XLA Modules:
  0.0 94.4 jit_solution(15500959156389634650)
XLA Ops:
  0.6 91.3 %window_attention.1 = (bf16[192,1024]{1,0:T(8,128)(2,1)}, bf16[192,1024]{1,0:T(8,128)(2,1)}, bf16[192,1024]{1,0:T(8,128)(2,1)}, bf16[192,1024]{1,0:T(8,128)(2,1)}) custom-call(bf16[192,1024]{1,0:T(8,128)(2,1)} %q_in.1, bf16[192,1024]{1,0:T(8,128)(2,1)} %k_in.1, bf16[192,1024]{1,0:T(8,128)(2,1)} %v_in.1, bf16[192,1024]{1,0:T(8,128)(2,1)} %g_in.1), custom_call_target="tpu_custom_call" | custom-call | flops 5435817984 | bytes 3145728 | tf_op jit(solution)/shard_map/window_attention/pallas_call | solution.py:560
  91.9 2.5 %store_results.1 = (bf16[192,1024]{1,0:T(8,128)(2,1)}, bf16[192,1024]{1,0:T(8,128)(2,1)}, bf16[192,1024]{1,0:T(8,128)(2,1)}, bf16[192,1024]{1,0:T(8,128)(2,1)}) custom-call(bf16[192,1024]{1,0:T(8,128)(2,1)} %get-tuple-element.8.refs_0_, bf16[192,1024]{1,0:T(8,128)(2,1)} %get-tuple-element.9.refs_1_, bf16[192,1024]{1,0:T(8,128)(2,1)} %get-tuple-element.10.refs_2_, ...), custom_call_target="tpu_custom_call" | custom-call | tf_op jit(solution)/shard_map/store_results/pallas_call | solution.py:602

commit v5 on v4

--- a/solution.py
+++ b/solution.py
@@ -442,6 +442,38 @@
         oq[n, :, 1] = dq.astype(BF16).reshape(HOPS, ROWS, DIM)
         rq_send(n, 3)
 
+    def left_out(n):
+        for to in range(2):
+            @pl.when(jnp.logical_not(relayed_to(n, to)))
+            def _():
+                kv_copy(n, to).wait_send()
+
+        @pl.when(jnp.logical_and(relays, among(n, TURN_RING)))
+        def _():
+            kv_forward_copy(n).wait_send()
+
+        for h in range(HOPS - 1):
+            @pl.when(qg_sends(n, h))
+            def _():
+                qg_copy(n, h).wait_send()
+
+        @pl.when(qg_crosses(n, 2))
+        def _():
+            qg_cross_copy(n, 2).wait_send()
+
+        @pl.when(qg_relayed(n))
+        def _():
+            qg_relay_copy(n).wait_send()
+
+        @pl.when(qg_passes(n))
+        def _():
+            qg_pass_copy(n).wait_send()
+
+        for delta in STAT_FROM:
+            @pl.when(exists(delta))
+            def _():
+                st_copy(n, delta).wait_send()
+
     def when_head(n, do, *rest):
         @pl.when(jnp.logical_and(n >= 0, n < HEADS))
         def _():
@@ -481,6 +513,7 @@
 
         when_head(t - 3, rq_pass, 2)
         when_head(t - 5, rq_pass, 1)
+        when_head(t - 5, left_out)
 
     @pl.loop(0, HEADS)
     def _(n):
@@ -505,7 +538,6 @@
         for to in range(2):
             @pl.when(jnp.logical_not(relayed_to(n, to)))
             def _():
-                kv_copy(n, to).wait_send()
                 rk_copy(n, to).wait_send()
 
             @pl.when(relayed_to(n, to))
@@ -514,38 +546,17 @@
 
         @pl.when(jnp.logical_and(relays, among(n, TURN_RING)))
         def _():
-            kv_forward_copy(n).wait_send()
             rk_forward_copy(n).wait_send()
 
-        for h in range(HOPS - 1):
-            @pl.when(qg_sends(n, h))
-            def _():
-                qg_copy(n, h).wait_send()
-
-            @pl.when(exists(h + 1))
-            def _():
-                rq_copy(n, h + 1).wait_send()
-        @pl.when(qg_crosses(n, 2))
-        def _():
-            qg_cross_copy(n, 2).wait_send()
-
-        @pl.when(qg_relayed(n))
-        def _():
-            qg_relay_copy(n).wait_send()
-
-        @pl.when(qg_passes(n))
-        def _():
-            qg_pass_copy(n).wait_send()
+        for h in range(1, HOPS):
+            @pl.when(exists(h))
+            def _():
+                rq_copy(n, h).wait_send()
 
         @pl.when(jnp.logical_and(rq_passes, among(n, TURN_RUN)))
         def _():
             for h in range(1, HOPS):
                 rq_over_copy(n, h).wait_send()
-
-        for delta in STAT_FROM:
-            @pl.when(exists(delta))
-            def _():
-                st_copy(n, delta).wait_send()
 
 
 def store(*refs):

time: 94.6 us -> 94.1 us (level)
  no operation moved by 1% of the time
where the time goes in v5:
time: 94.1 us; the launch traced here: 93.9 us
  Pallas kernels  93.3 us (99%)
    pallas_call x1, Pallas kernels, on_device(): pl.pallas_call(kernel, out_shape=(block,) * 4, in_specs=[pl.BlockSpec(mem...  90.8 us
    pallas_call x1, Pallas kernels, on_device(): pl.pallas_call(store, out_shape=(block,) * 4, in_specs=[vmem] * 4, out_sp...  2.51 us

profile of v5, /device:TPU:196, one launch (start us, length us, event | category | flops | bytes accessed | tf_op | source)
XLA Modules:
  0.0 93.9 jit_solution(8212535477873988323)
XLA Ops:
  0.6 90.8 %window_attention.1 = (bf16[192,1024]{1,0:T(8,128)(2,1)}, bf16[192,1024]{1,0:T(8,128)(2,1)}, bf16[192,1024]{1,0:T(8,128)(2,1)}, bf16[192,1024]{1,0:T(8,128)(2,1)}) custom-call(bf16[192,1024]{1,0:T(8,128)(2,1)} %q_in.1, bf16[192,1024]{1,0:T(8,128)(2,1)} %k_in.1, bf16[192,1024]{1,0:T(8,128)(2,1)} %v_in.1, bf16[192,1024]{1,0:T(8,128)(2,1)} %g_in.1), custom_call_target="tpu_custom_call" | custom-call | flops 5435817984 | bytes 3145728 | tf_op jit(solution)/shard_map/window_attention/pallas_call | solution.py:571
  91.4 2.5 %store_results.1 = (bf16[192,1024]{1,0:T(8,128)(2,1)}, bf16[192,1024]{1,0:T(8,128)(2,1)}, bf16[192,1024]{1,0:T(8,128)(2,1)}, bf16[192,1024]{1,0:T(8,128)(2,1)}) custom-call(bf16[192,1024]{1,0:T(8,128)(2,1)} %get-tuple-element.8.refs_0_, bf16[192,1024]{1,0:T(8,128)(2,1)} %get-tuple-element.9.refs_1_, bf16[192,1024]{1,0:T(8,128)(2,1)} %get-tuple-element.10.refs_2_, ...), custom_call_target="tpu_custom_call" | custom-call | tf_op jit(solution)/shard_map/store_results/pallas_call | solution.py:613
